TPU v7x, 32 devices: a whole 2x2x4 slice. The times are simulated.
32 devices in a mesh: tensor: 4 (over y, core), batch: 8 (over z, x).
Axes of the slice: x: 2, y: 2, z: 4, core: 2. Of those that a mesh axis runs over, the one named last changes fastest.
Arguments:
- layer_in: bfloat16 [3, 4096, 1024], P(None, 'batch', 'tensor'), may hold values from -6 to 6
- encoder_states: bfloat16 [4096, 1024], P('batch', 'tensor'), may hold values from -6 to 6
- w_self: bfloat16 [3, 1024, 1024], P(None, None, 'tensor'), may hold values from -0.1875 to 0.1875
- w_rel: bfloat16 [1024, 512], P(None, 'tensor'), may hold values from -0.1875 to 0.1875
- w_cross: bfloat16 [3, 1024, 1024], P(None, None, 'tensor'), may hold values from -0.1875 to 0.1875
- w_attn_out: bfloat16 [2, 1024, 1024], P(None, 'tensor'), may hold values from -0.75 to 0.75
- w_in: bfloat16 [1024, 4096], P(None, 'tensor'), may hold values from -0.1875 to 0.1875
- w_out: bfloat16 [4096, 1024], P('tensor'), may hold values from -0.09375 to 0.09375
- proj_bias: float32 [4, 1024], P(None, 'tensor'), may hold values from -3 to 3
- rel_bias: float32 [512], P('tensor'), may hold values from -4 to 4
- ffn_in_bias: float32 [4096], P('tensor'), may hold values from -3 to 3
- out_bias: float32 [3, 1024], P(None, 'tensor'), may hold values from -0.7 to 10.7
- norm_gain: float32 [3, 1024], P(None, 'tensor'), may hold values from 0.5 to 1.5
- norm_bias: float32 [3, 1024], P(None, 'tensor'), may hold values from -2 to 2
- rel_buckets: int32 [512], replicated, may hold values from 0 to 31
- slot_log: int32 [8], P('batch'), may hold values from 0 to 2
- tgt_fill: int32 [8, 4], P('batch'), may hold values from 0 to 511
- enc_fill: int32 [8, 4], P('batch'), may hold values from 0 to 511
- out_grad: bfloat16 [3, 4096, 1024], P(None, 'batch', 'tensor'), may hold values from -6 to 6
Outputs:
- layer_out: bfloat16 [3, 4096, 1024], P(None, 'batch', 'tensor')
- grad_layer_in: float32 [3, 4096, 1024], P(None, 'batch', 'tensor')
- grad_encoder: float32 [4096, 1024], P('batch', 'tensor')
- grad_w_self: float32 [3, 1024, 1024], P(None, 'batch', 'tensor')
- grad_w_rel: float32 [1024, 512], P('batch', 'tensor')
- grad_w_cross: float32 [3, 1024, 1024], P(None, 'batch', 'tensor')
- grad_w_attn_out: float32 [2, 1024, 1024], P(None, 'tensor', 'batch')
- grad_w_in: float32 [1024, 4096], P('batch', 'tensor')
- grad_w_out: float32 [4096, 1024], P('tensor', 'batch')
- grad_proj_bias: float32 [4, 1024], P(None, ('tensor', 'batch'))
- grad_rel_bias: float32 [512], P(('tensor', 'batch'))
- grad_ffn_in_bias: float32 [4096], P(('tensor', 'batch'))
- grad_out_bias: float32 [3, 1024], P(None, ('tensor', 'batch'))
- grad_norm_gain: float32 [3, 1024], P(None, ('tensor', 'batch'))
- grad_norm_bias: float32 [3, 1024], P(None, ('tensor', 'batch'))
All inputs are finite; a program needn't handle non-finite values.
Results may differ from a plain program's by a relative error of at most 0.033.
Values may be sent and summed in bfloat16 or wider, within the bound.
A program may use at most 192 MiB of HBM per device.

v0:
```python
import jax
import jax.numpy as jnp
from jax import lax
from jax.sharding import PartitionSpec as P

HEAD_DIM = 64


norm_eps = 1e-05
best = lax.Precision.HIGHEST
neg_big = -1e30


def grouping(code, span):
    place = jnp.arange(span, dtype=jnp.int32)
    width = jnp.right_shift(jnp.int32(span), code)
    return (place, place // width, width)


def layout(code, fill, span):
    place, group, width = grouping(code, span)
    half = jnp.maximum(width // 2, 1)
    lengths = width - fill % half
    valid = place % width < jnp.take(lengths, group)
    return (group, valid)


def lowered(v):
    return lax.optimization_barrier(v.astype(jnp.bfloat16)).astype(jnp.float32)


def gelu_exact(v):
    return jax.nn.gelu(v, approximate=False)


def widen(rows_part):
    return lax.all_gather(rows_part, "tensor", axis=2, tiled=True)


def narrow(partial_rows):
    return lax.psum_scatter(
        partial_rows.astype(jnp.bfloat16), "tensor", scatter_dimension=2, tiled=True
    ).astype(jnp.float32)


def project(rows, weight):
    return jnp.dot(rows, weight, preferred_element_type=jnp.float32)


def back_project(grad, weight):
    return jnp.einsum("ntk,ck->ntc", grad, weight, preferred_element_type=jnp.float32)


def weight_grad(rows, grad):
    return jnp.einsum("...c,...k->ck", rows, grad, preferred_element_type=jnp.float32)


def norm_forward(resid, gain, shift, width):
    mean = lax.psum(jnp.sum(resid, axis=-1), "tensor") / width
    centred = resid - mean[..., None]
    var = lax.psum(jnp.sum(centred * centred, axis=-1), "tensor") / width
    scale_rows = lax.rsqrt(var + norm_eps)[..., None]
    normed = centred * scale_rows
    return (normed * gain + shift, normed, scale_rows)


def norm_backward(grad_out, normed, scale_rows, gain, width):
    scaled = grad_out * gain
    plain_sum, cross_sum = lax.psum(
        (jnp.sum(scaled, axis=-1), jnp.sum(scaled * normed, axis=-1)), "tensor"
    )
    grad_in = scale_rows * (
        scaled - plain_sum[..., None] / width - normed * (cross_sum[..., None] / width)
    )
    return (grad_in, jnp.sum(grad_out * normed, axis=(0, 1)), jnp.sum(grad_out, axis=(0, 1)))


def self_scores(query, key, bias, own_bias, allowed_main, allowed_ahead, factor):
    raw = jnp.einsum("nthd,shd->nhts", query, key[0], preferred_element_type=jnp.float32)
    score = raw * factor + bias
    own = (
        jnp.einsum("nthd,nthd->nht", query[1:], key[1:], preferred_element_type=jnp.float32)
        * factor
        + own_bias
    )
    main = jnp.where(allowed_main, score[0], neg_big)
    ahead = jnp.where(allowed_ahead, score[1:], neg_big)
    return (main, ahead, own)


def self_forward(query, key, value, bias, own_bias, allowed_main, allowed_ahead, factor):
    main, ahead, own = self_scores(query, key, bias, own_bias, allowed_main, allowed_ahead, factor)
    top_main = jnp.max(main, axis=-1)
    weight_main = jnp.exp(main - top_main[..., None])
    total_main = jnp.sum(weight_main, axis=-1)
    top = jnp.maximum(jnp.max(ahead, axis=-1), own)
    weight = jnp.exp(ahead - top[..., None])
    weight_own = jnp.exp(own - top)
    total = jnp.sum(weight, axis=-1) + weight_own
    probs = jnp.concatenate(
        [(weight_main / total_main[..., None])[None], weight / total[..., None]], axis=0
    ).astype(jnp.bfloat16)
    mixed = jnp.einsum("nhts,shd->nthd", probs, value[0], preferred_element_type=jnp.float32)
    own_part = jnp.transpose(lowered(weight_own / total), (0, 2, 1))[..., None] * value[1:].astype(
        jnp.float32
    )
    att = jnp.concatenate([mixed[:1], mixed[1:] + own_part], axis=0).astype(jnp.bfloat16)
    lse = jnp.concatenate([(top_main + jnp.log(total_main))[None], top + jnp.log(total)], axis=0)
    return (att, lse)


def self_backward(
    query,
    key,
    value,
    grad_att,
    lse,
    bias,
    own_bias,
    allowed_main,
    allowed_ahead,
    factor,
    onehot,
    own_pick,
):
    main, ahead, own = self_scores(query, key, bias, own_bias, allowed_main, allowed_ahead, factor)
    prob = jnp.exp(jnp.concatenate([main[None], ahead], axis=0) - lse[..., None])
    prob_own = jnp.exp(own - lse[1:])
    grad_prob = jnp.einsum("nthd,shd->nhts", grad_att, value[0], preferred_element_type=jnp.float32)
    grad_own_prob = jnp.einsum(
        "nthd,nthd->nht", grad_att[1:], value[1:], preferred_element_type=jnp.float32
    )
    delta = jnp.sum(prob * grad_prob, axis=-1)
    delta = jnp.concatenate([delta[:1], delta[1:] + prob_own * grad_own_prob], axis=0)
    grad_score = prob * (grad_prob - delta[..., None])
    grad_own = prob_own * (grad_own_prob - delta[1:])
    own_low = jnp.transpose(lowered(prob_own), (0, 2, 1))[..., None]
    value_main = jnp.einsum(
        "nhts,nthd->shd", prob.astype(jnp.bfloat16), grad_att, preferred_element_type=jnp.float32
    )
    grad_value = jnp.concatenate(
        [value_main[None], own_low * grad_att[1:].astype(jnp.float32)], axis=0
    )
    score_low = (grad_score * factor).astype(jnp.bfloat16)
    own_score = jnp.transpose(lowered(grad_own * factor), (0, 2, 1))[..., None]
    grad_query = jnp.einsum("nhts,shd->nthd", score_low, key[0], preferred_element_type=jnp.float32)
    grad_query = jnp.concatenate(
        [grad_query[:1], grad_query[1:] + own_score * key[1:].astype(jnp.float32)], axis=0
    )
    key_main = jnp.einsum("nhts,nthd->shd", score_low, query, preferred_element_type=jnp.float32)
    grad_key = jnp.concatenate([key_main[None], own_score * query[1:].astype(jnp.float32)], axis=0)
    grad_rel = jnp.einsum("nhts,tsb->nthb", grad_score, onehot, precision=best)
    own_rel = jnp.transpose(grad_own, (0, 2, 1))[..., None] * own_pick
    grad_rel = jnp.concatenate([grad_rel[:1], grad_rel[1:] + own_rel], axis=0)
    return (grad_query, grad_key, grad_value, grad_rel)


def cross_scores(query, ckey, allowed, factor):
    raw = jnp.einsum("nthd,ehd->nhte", query, ckey, preferred_element_type=jnp.float32) * factor
    return jnp.where(allowed, raw, neg_big)


def cross_forward(query, ckey, cvalue, allowed, factor):
    score = cross_scores(query, ckey, allowed, factor)
    top = jnp.max(score, axis=-1)
    weight = jnp.exp(score - top[..., None])
    total = jnp.sum(weight, axis=-1)
    probs = (weight / total[..., None]).astype(jnp.bfloat16)
    mixed = jnp.einsum("nhte,ehd->nthd", probs, cvalue, preferred_element_type=jnp.float32).astype(
        jnp.bfloat16
    )
    return (mixed, top + jnp.log(total))


def cross_backward(query, ckey, cvalue, grad_mixed, lse, allowed, factor):
    prob = jnp.exp(cross_scores(query, ckey, allowed, factor) - lse[..., None])
    grad_prob = jnp.einsum("nthd,ehd->nhte", grad_mixed, cvalue, preferred_element_type=jnp.float32)
    grad_value = jnp.einsum(
        "nhte,nthd->ehd", prob.astype(jnp.bfloat16), grad_mixed, preferred_element_type=jnp.float32
    )
    grad_score = prob * (grad_prob - jnp.sum(prob * grad_prob, axis=-1, keepdims=True))
    score_low = (grad_score * factor).astype(jnp.bfloat16)
    grad_query = jnp.einsum("nhte,ehd->nthd", score_low, ckey, preferred_element_type=jnp.float32)
    grad_key = jnp.einsum("nhte,nthd->ehd", score_low, query, preferred_element_type=jnp.float32)
    return (grad_query, grad_key, grad_value)


def per_device(
    layer_in,
    encoder_states,
    w_self,
    w_rel,
    w_cross,
    w_attn_out,
    w_in,
    w_out,
    proj_bias,
    rel_bias,
    ffn_in_bias,
    out_bias,
    norm_gain,
    norm_bias,
    rel_buckets,
    slot_log,
    tgt_fill,
    enc_fill,
    out_grad,
):
    slabs = slot_log.shape[0]
    span = layer_in.shape[1] // slabs
    espan = encoder_states.shape[0] // slabs
    width = w_self.shape[1]
    heads_here = w_self.shape[2] // HEAD_DIM
    buckets = w_rel.shape[1] // heads_here
    factor = HEAD_DIM ** (-0.5)
    spots = jnp.arange(span, dtype=jnp.int32)
    gap = jnp.clip(spots[:, None] - spots[None, :], 0, span - 1)
    codes = jnp.arange(buckets, dtype=jnp.int32)
    onehot = (jnp.take(rel_buckets, gap)[..., None] == codes).astype(jnp.float32)
    own_pick = (codes == rel_buckets[0]).astype(jnp.float32)

    def slab_heads(v):
        return jnp.moveaxis(v.reshape(v.shape[0], slabs, span, heads_here, -1), 1, 0)

    def slab_rows(v):
        return jnp.moveaxis(v, 0, 1).reshape(v.shape[1], slabs * span, -1)

    def enc_heads(v):
        return v.reshape(slabs, espan, heads_here, -1)

    def enc_rows(v):
        return v.reshape(slabs * espan, -1)

    def self_masks(code, fill):
        group, valid = layout(code, fill, span)
        allowed = (group[:, None] == group[None, :]) & valid[None, :]
        return (
            allowed & (spots[:, None] >= spots[None, :]),
            allowed & (spots[:, None] > spots[None, :]),
        )

    def cross_mask(code, fill):
        group = grouping(code, span)[1]
        egroup, evalid = layout(code, fill, espan)
        return (group[:, None] == egroup[None, :]) & evalid[None, :]

    def rel_terms(rel):
        bias = jnp.einsum("nthb,tsb->nhts", rel, onehot, precision=best)
        own_bias = jnp.einsum("nthb,b->nht", rel[1:], own_pick, precision=best)
        return (bias, own_bias)

    def self_forward_slab(args):
        query, key, value, rel, code, fill = args
        allowed_main, allowed_ahead = self_masks(code, fill)
        bias, own_bias = rel_terms(rel)
        return self_forward(query, key, value, bias, own_bias, allowed_main, allowed_ahead, factor)

    def self_backward_slab(args):
        query, key, value, rel, grad_att, lse, code, fill = args
        allowed_main, allowed_ahead = self_masks(code, fill)
        bias, own_bias = rel_terms(rel)
        return self_backward(
            query,
            key,
            value,
            grad_att,
            lse,
            bias,
            own_bias,
            allowed_main,
            allowed_ahead,
            factor,
            onehot,
            own_pick,
        )

    def cross_forward_slab(args):
        query, ckey, cvalue, code, fill = args
        return cross_forward(query, ckey, cvalue, cross_mask(code, fill), factor)

    def cross_backward_slab(args):
        query, ckey, cvalue, grad_mixed, lse, code, fill = args
        return cross_backward(query, ckey, cvalue, grad_mixed, lse, cross_mask(code, fill), factor)

    full_input = widen(layer_in)

    def add_norm(prev, partial_rows, index):
        resid = prev + narrow(partial_rows) + out_bias[index]
        out, normed, scale_rows = norm_forward(resid, norm_gain[index], norm_bias[index], width)
        return (out, normed, scale_rows, widen(out.astype(jnp.bfloat16)), out)

    query = (project(full_input, w_self[0]) + proj_bias[0]).astype(jnp.bfloat16)
    key = project(full_input, w_self[1]).astype(jnp.bfloat16)
    value = (project(full_input, w_self[2]) + proj_bias[1]).astype(jnp.bfloat16)
    rel = project(full_input, w_rel) + rel_bias
    att_heads, self_lse = lax.map(
        self_forward_slab,
        (
            slab_heads(query),
            slab_heads(key),
            slab_heads(value),
            slab_heads(rel),
            slot_log,
            tgt_fill,
        ),
    )
    att = slab_rows(att_heads)
    first, first_normed, first_scale, first_full, first_all = add_norm(
        layer_in.astype(jnp.float32), project(att, w_attn_out[0]), 0
    )
    full_encoder = lax.all_gather(encoder_states, "tensor", axis=1, tiled=True)
    cquery = (project(first_full, w_cross[0]) + proj_bias[2]).astype(jnp.bfloat16)
    ckey = project(full_encoder, w_cross[1]).astype(jnp.bfloat16)
    cvalue = (project(full_encoder, w_cross[2]) + proj_bias[3]).astype(jnp.bfloat16)
    catt_heads, cross_lse = lax.map(
        cross_forward_slab,
        (slab_heads(cquery), enc_heads(ckey), enc_heads(cvalue), slot_log, enc_fill),
    )
    catt = slab_rows(catt_heads)
    second, second_normed, second_scale, second_full, second_all = add_norm(
        first, project(catt, w_attn_out[1]), 1
    )
    pre = project(second_full, w_in) + ffn_in_bias
    act = gelu_exact(pre).astype(jnp.bfloat16)
    third, third_normed, third_scale, third_full, third_all = add_norm(
        second, project(act, w_out), 2
    )
    result = third.astype(jnp.bfloat16)
    grad_third, gain_three, shift_three = norm_backward(
        out_grad.astype(jnp.float32), third_normed, third_scale, norm_gain[2], width
    )
    ffn_full = widen(grad_third.astype(jnp.bfloat16))
    grad_w_out = weight_grad(act, ffn_full)
    grad_act = back_project(ffn_full, w_out)
    grad_pre = jax.vjp(gelu_exact, pre)[1](grad_act)[0]
    pre_low = grad_pre.astype(jnp.bfloat16)
    grad_w_in = weight_grad(second_full, pre_low)
    ffn_bias_grad = jnp.sum(grad_pre, axis=(0, 1))
    bias_two = jnp.sum(grad_third, axis=(0, 1))
    grad_second_out = grad_third + narrow(back_project(pre_low, w_in))
    grad_second, gain_two, shift_two = norm_backward(
        grad_second_out, second_normed, second_scale, norm_gain[1], width
    )
    cross_full = widen(grad_second.astype(jnp.bfloat16))
    grad_out_one = weight_grad(catt, cross_full)
    grad_catt = back_project(cross_full, w_attn_out[1]).astype(jnp.bfloat16)
    bias_one = jnp.sum(grad_second, axis=(0, 1))
    cquery_heads, ckey_heads, cvalue_heads = lax.map(
        cross_backward_slab,
        (
            slab_heads(cquery),
            enc_heads(ckey),
            enc_heads(cvalue),
            slab_heads(grad_catt),
            cross_lse,
            slot_log,
            enc_fill,
        ),
    )
    grad_cquery = slab_rows(cquery_heads)
    grad_ckey = enc_rows(ckey_heads)
    grad_cvalue = enc_rows(cvalue_heads)
    cquery_low = grad_cquery.astype(jnp.bfloat16)
    ckey_low = grad_ckey.astype(jnp.bfloat16)
    cvalue_low = grad_cvalue.astype(jnp.bfloat16)
    grad_w_cross = jnp.stack(
        [
            weight_grad(first_full, cquery_low),
            weight_grad(full_encoder, ckey_low),
            weight_grad(full_encoder, cvalue_low),
        ]
    )
    encoder_terms = jnp.einsum(
        "ek,ck->ec", ckey_low, w_cross[1], preferred_element_type=jnp.float32
    ) + jnp.einsum("ek,ck->ec", cvalue_low, w_cross[2], preferred_element_type=jnp.float32)
    grad_encoder = lax.psum_scatter(
        encoder_terms.astype(jnp.bfloat16), "tensor", scatter_dimension=1, tiled=True
    ).astype(jnp.float32)
    grad_first_out = grad_second + narrow(back_project(cquery_low, w_cross[0]))
    grad_first, gain_one, shift_one = norm_backward(
        grad_first_out, first_normed, first_scale, norm_gain[0], width
    )
    self_full = widen(grad_first.astype(jnp.bfloat16))
    grad_out_zero = weight_grad(att, self_full)
    grad_att = back_project(self_full, w_attn_out[0]).astype(jnp.bfloat16)
    bias_zero = jnp.sum(grad_first, axis=(0, 1))
    query_heads, key_heads, value_heads, rel_heads = lax.map(
        self_backward_slab,
        (
            slab_heads(query),
            slab_heads(key),
            slab_heads(value),
            slab_heads(rel),
            slab_heads(grad_att),
            self_lse,
            slot_log,
            tgt_fill,
        ),
    )
    grad_query = slab_rows(query_heads)
    grad_key = slab_rows(key_heads)
    grad_value = slab_rows(value_heads)
    grad_rel = slab_rows(rel_heads)
    query_low = grad_query.astype(jnp.bfloat16)
    key_low = grad_key.astype(jnp.bfloat16)
    value_low = grad_value.astype(jnp.bfloat16)
    rel_low = grad_rel.astype(jnp.bfloat16)
    grad_w_self = jnp.stack(
        [
            weight_grad(full_input, query_low),
            weight_grad(full_input, key_low),
            weight_grad(full_input, value_low),
        ]
    )
    grad_w_rel = weight_grad(full_input, rel_low)
    input_terms = (
        back_project(query_low, w_self[0])
        + back_project(key_low, w_self[1])
        + back_project(value_low, w_self[2])
        + back_project(rel_low, w_rel)
    )
    grad_input = grad_first + narrow(input_terms)
    grad_w_attn = jnp.stack([grad_out_zero, grad_out_one])
    proj_bias_grad = jnp.stack(
        [
            jnp.sum(grad_query, axis=(0, 1)),
            jnp.sum(grad_value, axis=(0, 1)),
            jnp.sum(grad_cquery, axis=(0, 1)),
            jnp.sum(grad_cvalue, axis=0),
        ]
    )
    rel_bias_grad = jnp.sum(grad_rel, axis=(0, 1))
    out_bias_grad = jnp.stack([bias_zero, bias_one, bias_two])
    gain_grad = jnp.stack([gain_one, gain_two, gain_three])
    shift_grad = jnp.stack([shift_one, shift_two, shift_three])
    sent = (
        lax.psum_scatter(grad_w_self, "batch", scatter_dimension=1, tiled=True),
        lax.psum_scatter(grad_w_rel, "batch", scatter_dimension=0, tiled=True),
        lax.psum_scatter(grad_w_cross, "batch", scatter_dimension=1, tiled=True),
        lax.psum_scatter(grad_w_attn, "batch", scatter_dimension=2, tiled=True),
        lax.psum_scatter(grad_w_in, "batch", scatter_dimension=0, tiled=True),
        lax.psum_scatter(grad_w_out, "batch", scatter_dimension=1, tiled=True),
        lax.psum_scatter(proj_bias_grad, "batch", scatter_dimension=1, tiled=True),
        lax.psum_scatter(rel_bias_grad, "batch", scatter_dimension=0, tiled=True),
        lax.psum_scatter(ffn_bias_grad, "batch", scatter_dimension=0, tiled=True),
        lax.psum_scatter(out_bias_grad, "batch", scatter_dimension=1, tiled=True),
        lax.psum_scatter(gain_grad, "batch", scatter_dimension=1, tiled=True),
        lax.psum_scatter(shift_grad, "batch", scatter_dimension=1, tiled=True),
    )
    return (result, grad_input, grad_encoder) + tuple(sent)


def solution(mesh):
    return jax.shard_map(
        per_device,
        mesh=mesh,
        in_specs=(
            P(None, "batch", "tensor"),
            P("batch", "tensor"),
            P(None, None, "tensor"),
            P(None, "tensor"),
            P(None, None, "tensor"),
            P(None, "tensor", None),
            P(None, "tensor"),
            P("tensor", None),
            P(None, "tensor"),
            P("tensor"),
            P("tensor"),
            P(None, "tensor"),
            P(None, "tensor"),
            P(None, "tensor"),
            P(),
            P("batch"),
            P("batch", None),
            P("batch", None),
            P(None, "batch", "tensor"),
        ),
        out_specs=(
            P(None, "batch", "tensor"),
            P(None, "batch", "tensor"),
            P("batch", "tensor"),
            P(None, "batch", "tensor"),
            P("batch", "tensor"),
            P(None, "batch", "tensor"),
            P(None, "tensor", "batch"),
            P("batch", "tensor"),
            P("tensor", "batch"),
            P(None, ("tensor", "batch")),
            P(("tensor", "batch")),
            P(("tensor", "batch")),
            P(None, ("tensor", "batch")),
            P(None, ("tensor", "batch")),
            P(None, ("tensor", "batch")),
        ),
        check_vma=False,
    )
```

profile of v0, /device:TPU:0, one launch (start us, length us, event | category | flops | bytes accessed | tf_op | source)
XLA Modules:
  0.0 4230.5 jit_solution(8813312656843986199)
XLA Ops:
  9.8 2754.6 %gather_fusion = s32[262144]{0:T(1024)} fusion(s32[512]{0:T(512)S(1)} %copy-done.1, s32[262144]{0:T(1024)S(1)} %broadcast_clamp_fusion), kind=kCustom, calls=%fused_computation | custom fusion | bytes 3145728 | tf_op jit(solution)/shard_map/jit(_take)/gather | solution.py:219
  2789.3 18.9 fusion.4
  2864.5 38.3 reduce-scatter.26.cloned.1.call-done
  2926.0 26.6 all-gather.12.cloned.1.call-done
  2970.6 38.0 reduce-scatter.28.cloned.1.call-done
  3028.5 30.2 all-gather.14.cloned.1.call-done
  3066.0 15.4 multiply_convert_fusion.1
  3087.9 38.0 reduce-scatter.30.cloned.1.call-done
  3167.2 29.2 all-gather.16.cloned.1.call-done
  3215.4 38.1 reduce-scatter.32.cloned.1.call-done
  3274.1 28.2 all-gather.18.cloned.1.call-done
  3312.4 18.5 fusion.13
  3338.9 38.0 reduce-scatter.34.cloned.1.call-done
  3473.8 22.4 fusion.2
  3580.5 61.7 %reduce-scatter.56.cloned.1.call-done = f32[32,3]{1,0:T(8,128)} async-done(((f32[256,3]{1,0:T(8,128)}), f32[32,3]{1,0:T(8,128)}) %reduce-scatter.56.cloned.1.call-update) | async-done | bytes 400
  3644.7 19.8 all-reduce.2
  3665.7 39.7 reduce-scatter.52.cloned.1.call-done
  3706.7 63.3 %reduce-scatter.42.cloned.1.call-done = f32[128,128]{0,1:T(8,128)} async-done(((f32[1024,128]{0,1:T(8,128)}), f32[128,128]{0,1:T(8,128)}) %reduce-scatter.42.cloned.1.call-update) | async-done | bytes 65552 | tf_op jit(solution)/shard_map/reduce_scatter | solution.py:438
  3771.6 76.5 %reduce-scatter.40.cloned.1.call-done = f32[3,128,256]{1,2,0:T(8,128)} async-done(((f32[3,1024,256]{1,2,0:T(8,128)}), f32[3,128,256]{1,2,0:T(8,128)}) %reduce-scatter.40.cloned.1.call-update) | async-done | bytes 393232 | tf_op jit(solution)/shard_map/reduce_scatter | solution.py:437
  3850.0 37.7 reduce-scatter.36.cloned.1.call-done
  3890.6 89.8 %reduce-scatter.50.cloned.1.call-done = f32[1024,128]{1,0:T(8,128)} async-done(((f32[1024,1024]{1,0:T(8,128)}), f32[1024,128]{1,0:T(8,128)}) %reduce-scatter.50.cloned.1.call-update) | async-done | bytes 524304 | tf_op jit(solution)/shard_map/reduce_scatter | solution.py:442
  3980.4 92.5 %reduce-scatter.48.cloned.1.call-done = f32[128,1024]{1,0:T(8,128)} async-done(((f32[1024,1024]{1,0:T(8,128)}), f32[128,1024]{1,0:T(8,128)}) %reduce-scatter.48.cloned.1.call-update) | async-done | bytes 524304 | tf_op jit(solution)/shard_map/reduce_scatter | solution.py:441
  4072.9 78.8 %reduce-scatter.44.cloned.1.call-done = f32[3,128,256]{2,1,0:T(8,128)} async-done(((f32[3,1024,256]{2,1,0:T(8,128)}), f32[3,128,256]{2,1,0:T(8,128)}) %reduce-scatter.44.cloned.1.call-update) | async-done | bytes 393232 | tf_op jit(solution)/shard_map/reduce_scatter | solution.py:439
  4151.7 71.5 %reduce-scatter.46.cloned.1.call-done = f32[2,256,128]{2,1,0:T(8,128)} async-done(((f32[2,256,1024]{2,1,0:T(8,128)}), f32[2,256,128]{2,1,0:T(8,128)}) %reduce-scatter.46.cloned.1.call-update) | async-done | bytes 262160 | tf_op jit(solution)/shard_map/reduce_scatter | solution.py:440
  (412 shorter events, 446.6 us)
Async XLA Ops:
  7.2 2767.9 %all-gather.8.cloned.1.call-start = ((), (), s32[]{:S(2)}) async-start(), calls=%async_computation.17 | async-start | bytes 3932160 | tf_op jit(solution)/shard_map/all_gather | solution.py:37
  7.9 2894.8 %reduce-scatter.26.cloned.1.call-start = ((), (), s32[]{:S(2)}) async-start(), calls=%async_computation.18 | async-start | bytes 3932160 | tf_op jit(solution)/shard_map/reduce_scatter | solution.py:41
  2862.0 59.6 %all-gather.10.cloned.1.call-start = ((), (), s32[]{:S(2)}) async-start(), calls=%async_computation.19 | async-start | bytes 1310720 | tf_op jit(solution)/shard_map/all_gather | solution.py:311
  2862.7 89.9 %all-gather.12.cloned.1.call-start = ((), (), s32[]{:S(2)}) async-start(), calls=%async_computation.20 | async-start | bytes 3932160 | tf_op jit(solution)/shard_map/all_gather | solution.py:37
  2920.8 87.8 %reduce-scatter.28.cloned.1.call-start = ((), (), s32[]{:S(2)}) async-start(), calls=%async_computation.21 | async-start | bytes 3932160 | tf_op jit(solution)/shard_map/reduce_scatter | solution.py:41
  2970.6 88.1 %all-gather.14.cloned.1.call-start = ((), (), s32[]{:S(2)}) async-start(), calls=%async_computation.22 | async-start | bytes 3932160 | tf_op jit(solution)/shard_map/all_gather | solution.py:37
  3028.3 97.7 %reduce-scatter.30.cloned.1.call-start = ((), (), s32[]{:S(2)}) async-start(), calls=%async_computation.23 | async-start | bytes 3932160 | tf_op jit(solution)/shard_map/reduce_scatter | solution.py:41
  3087.8 108.5 %all-gather.16.cloned.1.call-start = ((), (), s32[]{:S(2)}) async-start(), calls=%async_computation.24 | async-start | bytes 3932160 | tf_op jit(solution)/shard_map/all_gather | solution.py:37
  3166.9 86.6 %reduce-scatter.32.cloned.1.call-start = ((), (), s32[]{:S(2)}) async-start(), calls=%async_computation.25 | async-start | bytes 3932160 | tf_op jit(solution)/shard_map/reduce_scatter | solution.py:41
  3215.4 86.8 %all-gather.18.cloned.1.call-start = ((), (), s32[]{:S(2)}) async-start(), calls=%async_computation.26 | async-start | bytes 3932160 | tf_op jit(solution)/shard_map/all_gather | solution.py:37
  3273.0 103.9 %reduce-scatter.34.cloned.1.call-start = ((), (), s32[]{:S(2)}) async-start(), calls=%async_computation.27 | async-start | bytes 3932160 | tf_op jit(solution)/shard_map/reduce_scatter | solution.py:41
  3338.8 85.6 %all-gather.20.cloned.1.call-start = ((), (), s32[]{:S(2)}) async-start(), calls=%async_computation.28 | async-start | bytes 3932160 | tf_op jit(solution)/shard_map/all_gather | solution.py:37
  3394.2 177.0 %reduce-scatter.38.cloned.1.call-start = ((), (), s32[]{:S(2)}) async-start(), calls=%async_computation.30 | async-start | bytes 1310720 | tf_op jit(solution)/shard_map/reduce_scatter | solution.py:376
  3409.8 163.3 %reduce-scatter.54.cloned.1.call-start = ((), (), s32[]{:S(2)}) async-start(), calls=%async_computation.38 | async-start | bytes 147456
  3414.3 164.9 %reduce-scatter.58.cloned.1.call-start = ((), (), s32[]{:S(2)}) async-start(), calls=%async_computation.40 | async-start | bytes 147456
  3415.2 227.0 %reduce-scatter.56.cloned.1.call-start = ((), (), s32[]{:S(2)}) async-start(), calls=%async_computation.39 | async-start | bytes 147456
  3416.1 289.3 %reduce-scatter.52.cloned.1.call-start = ((), (), s32[]{:S(2)}) async-start(), calls=%async_computation.37 | async-start | bytes 147456
  3516.6 253.4 %reduce-scatter.42.cloned.1.call-start = ((), (), s32[]{:S(2)}) async-start(), calls=%async_computation.32 | async-start | bytes 589824 | tf_op jit(solution)/shard_map/reduce_scatter | solution.py:438
  3522.2 325.9 %reduce-scatter.40.cloned.1.call-start = ((), (), s32[]{:S(2)}) async-start(), calls=%async_computation.31 | async-start | bytes 3538944 | tf_op jit(solution)/shard_map/reduce_scatter | solution.py:437
  3529.6 358.1 %reduce-scatter.36.cloned.1.call-start = ((), (), s32[]{:S(2)}) async-start(), calls=%async_computation.29 | async-start | bytes 3932160 | tf_op jit(solution)/shard_map/reduce_scatter | solution.py:41
  3539.2 441.3 %reduce-scatter.50.cloned.1.call-start = ((), (), s32[]{:S(2)}) async-start(), calls=%async_computation.36 | async-start | bytes 4718592 | tf_op jit(solution)/shard_map/reduce_scatter | solution.py:442
  3547.8 525.1 %reduce-scatter.48.cloned.1.call-start = ((), (), s32[]{:S(2)}) async-start(), calls=%async_computation.35 | async-start | bytes 4718592 | tf_op jit(solution)/shard_map/reduce_scatter | solution.py:441
  3556.2 595.6 %reduce-scatter.44.cloned.1.call-start = ((), (), s32[]{:S(2)}) async-start(), calls=%async_computation.33 | async-start | bytes 3538944 | tf_op jit(solution)/shard_map/reduce_scatter | solution.py:439
  3562.6 660.6 %reduce-scatter.46.cloned.1.call-start = ((), (), s32[]{:S(2)}) async-start(), calls=%async_computation.34 | async-start | bytes 2359296 | tf_op jit(solution)/shard_map/reduce_scatter | solution.py:440
  (85 other events, 12488.6 us)
Sparse Core Ops, SparseCore 0:
  9.6 31.6 all-gather.7
  2862.1 40.6 reduce-scatter.25
  2904.4 17.1 all-gather.9
  2923.6 28.9 all-gather.11
  2970.7 37.9 reduce-scatter.27
  3028.4 30.2 all-gather.13
  3088.0 37.9 reduce-scatter.29
  3167.0 29.2 all-gather.15
  3215.5 37.9 reduce-scatter.31
  3273.1 29.0 all-gather.17
  3338.9 37.9 reduce-scatter.33
  3394.4 29.9 all-gather.19
  3427.1 24.8 reduce-scatter.37
  3455.2 60.8 reduce-scatter.53
  3519.2 59.8 reduce-scatter.57
  3582.3 59.8 reduce-scatter.55
  3645.4 59.9 reduce-scatter.51
  3708.6 61.4 reduce-scatter.41
  3774.1 73.9 reduce-scatter.39
  3850.6 37.0 reduce-scatter.35
  3891.9 88.4 reduce-scatter.49
  3985.1 87.7 reduce-scatter.47
  4077.1 74.5 reduce-scatter.43
  4155.7 67.4 reduce-scatter.45
where the time goes:
time: 4240 us; the launch traced here: 4230 us
  local copies, waits for them, and re-layouts  2840 us (67%)
  waiting for transfers between devices  931 us (22%)
  matrix products  206 us (5%)
  other arithmetic  141 us (3%)
  blocking collectives  90.3 us (2%)
    gather x2, local copies, waits for them, and re-layouts, per_device(): jnp.take(rel_buckets, gap)[..., None] == codes  2760 us
    reduce_scatter x6, waiting for transfers between devices, narrow(): lax.psum_scatter(partial_rows.astype(jnp.bfloat16), 'tensor', scatter_dim...  228 us
    all_gather x6, waiting for transfers between devices, widen(): return lax.all_gather(rows_part, 'tensor', axis=2, tiled=True)  122 us
    unnamed x28, waiting for transfers between devices  108 us
    reduce_scatter x1, waiting for transfers between devices, per_device(): lax.psum_scatter(grad_w_in, 'batch', scatter_dimension=0, tiled=True)  92.5 us
    reduce_scatter x1, waiting for transfers between devices, per_device(): lax.psum_scatter(grad_w_out, 'batch', scatter_dimension=1, tiled=True)  89.8 us
  transfers between devices with their start and end apart: 24, of which 21 were waited for; matrix products, arithmetic and copies ran while one was open for 70% of the time, Pallas kernels for 0%

commit v1 on v0

--- a/solution.py
+++ b/solution.py
@@ -214,9 +214,13 @@
     buckets = w_rel.shape[1] // heads_here
     factor = HEAD_DIM ** (-0.5)
     spots = jnp.arange(span, dtype=jnp.int32)
-    gap = jnp.clip(spots[:, None] - spots[None, :], 0, span - 1)
     codes = jnp.arange(buckets, dtype=jnp.int32)
-    onehot = (jnp.take(rel_buckets, gap)[..., None] == codes).astype(jnp.float32)
+    lap = 2 * span
+    turned = jnp.concatenate(
+        [rel_buckets[:1], jnp.broadcast_to(rel_buckets[:1], (span,)), rel_buckets[:0:-1]]
+    )
+    table = jnp.tile(turned, span)[: span * (lap - 1)].reshape(span, lap - 1)[:, :span]
+    onehot = (table[..., None] == codes).astype(jnp.float32)
     own_pick = (codes == rel_buckets[0]).astype(jnp.float32)
 
     def slab_heads(v):
@@ -433,13 +437,16 @@
     out_bias_grad = jnp.stack([bias_zero, bias_one, bias_two])
     gain_grad = jnp.stack([gain_one, gain_two, gain_three])
     shift_grad = jnp.stack([shift_one, shift_two, shift_three])
+    def shared(part, axis, **how):
+        return lax.psum_scatter(part.astype(jnp.bfloat16), axis, **how).astype(jnp.float32)
+
     sent = (
-        lax.psum_scatter(grad_w_self, "batch", scatter_dimension=1, tiled=True),
-        lax.psum_scatter(grad_w_rel, "batch", scatter_dimension=0, tiled=True),
-        lax.psum_scatter(grad_w_cross, "batch", scatter_dimension=1, tiled=True),
-        lax.psum_scatter(grad_w_attn, "batch", scatter_dimension=2, tiled=True),
-        lax.psum_scatter(grad_w_in, "batch", scatter_dimension=0, tiled=True),
-        lax.psum_scatter(grad_w_out, "batch", scatter_dimension=1, tiled=True),
+        shared(grad_w_self, "batch", scatter_dimension=1, tiled=True),
+        shared(grad_w_rel, "batch", scatter_dimension=0, tiled=True),
+        shared(grad_w_cross, "batch", scatter_dimension=1, tiled=True),
+        shared(grad_w_attn, "batch", scatter_dimension=2, tiled=True),
+        shared(grad_w_in, "batch", scatter_dimension=0, tiled=True),
+        shared(grad_w_out, "batch", scatter_dimension=1, tiled=True),
         lax.psum_scatter(proj_bias_grad, "batch", scatter_dimension=1, tiled=True),
         lax.psum_scatter(rel_bias_grad, "batch", scatter_dimension=0, tiled=True),
         lax.psum_scatter(ffn_bias_grad, "batch", scatter_dimension=0, tiled=True),

time: 4240 us -> 1430 us (0.34)
  local copies, waits for them, and re-layouts: 2840 us -> 106 us
  waiting for transfers between devices: 931 us -> 877 us
    gather x2 -> x0, local copies, waits for them, and re-layouts: 2760 us -> none  [per_device(): jnp.take(rel_buckets, gap)[..., None] == codes]
    reduce_scatter x6 -> x2, waiting for transfers between devices: 472 us -> 78.1 us  [shared(): lax.psum_scatter(part.astype(jnp.bfloat16), axis, **how).astype(jnp.float32)]
    unnamed x28 -> x32, waiting for transfers between devices: 108 us -> 421 us
  transfers between devices with their start and end apart: 24 -> 24, of which waited for: 21 -> 22; matrix products, arithmetic and copies ran while one was open for 70% -> 14% of each run, Pallas kernels for 0% -> 0%
where the time goes in v1:
time: 1430 us; the launch traced here: 1420 us
  waiting for transfers between devices  877 us (61%)
  matrix products  199 us (14%)
  other arithmetic  129 us (9%)
  local copies, waits for them, and re-layouts  106 us (7%)
  blocking collectives  87.9 us (6%)
  between operations  18.2 us (1%)
    unnamed x32, waiting for transfers between devices  421 us
    reduce_scatter x6, waiting for transfers between devices, narrow(): lax.psum_scatter(partial_rows.astype(jnp.bfloat16), 'tensor', scatter_dim...  225 us
    all_gather x6, waiting for transfers between devices, widen(): return lax.all_gather(rows_part, 'tensor', axis=2, tiled=True)  128 us
    reduce_scatter x2, waiting for transfers between devices, shared(): lax.psum_scatter(part.astype(jnp.bfloat16), axis, **how).astype(jnp.float32)  78.1 us
    unnamed x222, local copies, waits for them, and re-layouts  51.6 us
    dot_general x9, matrix products, back_project(): jnp.einsum('ntk,ck->ntc', grad, weight, preferred_element_type=jnp.float32)  34.3 us
    psum x3, blocking collectives, norm_backward(): lax.psum((jnp.sum(scaled, axis=-1), jnp.sum(scaled * normed, axis=-1)), '...  32.6 us
    dot_general x11, matrix products, project(): return jnp.dot(rows, weight, preferred_element_type=jnp.float32)  32.4 us
  transfers between devices with their start and end apart: 24, of which 22 were waited for; matrix products, arithmetic and copies ran while one was open for 14% of the time, Pallas kernels for 0%

profile of v1, /device:TPU:0, one launch (start us, length us, event | category | flops | bytes accessed | tf_op | source)
XLA Modules:
  0.0 1419.3 jit_solution(9813260554133438818)
XLA Ops:
  56.5 18.9 %fusion.4 = f32[512,512,3,4]{1,3,2,0:T(4,128)} fusion(f32[3,512,4,32]{3,2,0,1:T(4,128)} %copy.255, s32[512,512]{1,0:T(8,128)} %slice.264), kind=kOutput, calls=%fused_computation.4 | convolution fusion | flops 1216348160 | bytes 14417920 | tf_op jit(solution)/shard_map/while/body/eval_jaxpr/nthb,tsb->nhts/dot_general | solution.py:252
  129.7 35.6 %reduce-scatter.34.cloned.1.call-done = bf16[3,512,256]{2,1,0:T(8,128)(2,1)} async-done(((bf16[3,512,1024]{2,1,0:T(8,128)(2,1)}), bf16[3,512,256]{2,1,0:T(8,128)(2,1)}) %reduce-scatter.34.cloned.1.call-update) | async-done | bytes 786448 | tf_op jit(solution)/shard_map/reduce_scatter | solution.py:41
  188.4 26.6 %all-gather.12.cloned.1.call-done = bf16[3,512,1024]{2,1,0:T(8,128)(2,1)} async-done(((bf16[3,512,256]{2,1,0:T(8,128)(2,1)}), bf16[3,512,1024]{2,1,0:T(8,128)(2,1)}) %all-gather.12.cloned.1.call-update) | async-done | bytes 3145744 | tf_op jit(solution)/shard_map/all_gather | solution.py:37
  233.2 38.1 %reduce-scatter.36.cloned.1.call-done = bf16[3,512,256]{2,1,0:T(8,128)(2,1)} async-done(((bf16[3,512,1024]{2,1,0:T(8,128)(2,1)}), bf16[3,512,256]{2,1,0:T(8,128)(2,1)}) %reduce-scatter.36.cloned.1.call-update) | async-done | bytes 786448 | tf_op jit(solution)/shard_map/reduce_scatter | solution.py:41
  290.9 30.5 %all-gather.14.cloned.1.call-done = bf16[3,512,1024]{2,1,0:T(8,128)(2,1)} async-done(((bf16[3,512,256]{2,1,0:T(8,128)(2,1)}), bf16[3,512,1024]{2,1,0:T(8,128)(2,1)}) %all-gather.14.cloned.1.call-update) | async-done | bytes 3145744 | tf_op jit(solution)/shard_map/all_gather | solution.py:37
  328.6 15.6 %multiply_convert_fusion.1 = (bf16[3,512,1024]{2,1,0:T(8,128)(2,1)S(1)}, f32[3,512,1024]{2,1,0:T(8,128)}) fusion(f32[3,512,1024]{2,1,0:T(8,128)S(1)} %get-tuple-element.323, f32[1024]{0:T(1024)S(1)} %copy-done.73, u8[512,1024]{1,0:T(8,128)(4,1)S(1)} %get-tuple-element.233, u8[512,1024]{1,0:T(8,128)(4,1)S(1)} %get-tuple-element.232), kind=kLoop, calls=%fused_computation.51 | loop fusion | flops 111673344 | bytes 16781312 | tf_op jit(solution)/shard_map/convert_element_type | solution.py:328
  350.8 38.0 %reduce-scatter.38.cloned.1.call-done = bf16[3,512,256]{2,1,0:T(8,128)(2,1)} async-done(((bf16[3,512,1024]{2,1,0:T(8,128)(2,1)}), bf16[3,512,256]{2,1,0:T(8,128)(2,1)}) %reduce-scatter.38.cloned.1.call-update) | async-done | bytes 786448 | tf_op jit(solution)/shard_map/reduce_scatter | solution.py:41
  426.5 28.6 %all-gather.16.cloned.1.call-done = bf16[3,512,1024]{2,1,0:T(8,128)(2,1)} async-done(((bf16[3,512,256]{2,1,0:T(8,128)(2,1)}), bf16[3,512,1024]{2,1,0:T(8,128)(2,1)}) %all-gather.16.cloned.1.call-update) | async-done | bytes 3145744 | tf_op jit(solution)/shard_map/all_gather | solution.py:37
  474.3 38.0 %reduce-scatter.40.cloned.1.call-done = bf16[3,512,256]{2,1,0:T(8,128)(2,1)} async-done(((bf16[3,512,1024]{2,1,0:T(8,128)(2,1)}), bf16[3,512,256]{2,1,0:T(8,128)(2,1)}) %reduce-scatter.40.cloned.1.call-update) | async-done | bytes 786448 | tf_op jit(solution)/shard_map/reduce_scatter | solution.py:41
  528.9 29.9 %all-gather.18.cloned.1.call-done = bf16[3,512,1024]{2,1,0:T(8,128)(2,1)} async-done(((bf16[3,512,256]{2,1,0:T(8,128)(2,1)}), bf16[3,512,1024]{2,1,0:T(8,128)(2,1)}) %all-gather.18.cloned.1.call-update) | async-done | bytes 3145744 | tf_op jit(solution)/shard_map/all_gather | solution.py:37
  568.2 18.5 %fusion.13 = bf16[3,4,512,512]{2,3,0,1:T(8,128)(2,1)S(1)} fusion(f32[4,512,3,512]{3,1,2,0:T(8,128)} %fusion.113, f32[3,4,512]{2,0,1:T(4,128)S(1)} %log_add_fusion, f32[4,512,3,512]{3,1,2,0:T(8,128)} %copy-done.5, pred[512,512]{0,1:T(8,128)(4,1)S(1)} %get-tuple-element.312), kind=kOutput, calls=%fused_computation.17 | output fusion | flops 34609664 | bytes 31744000 | tf_op jit(solution)/shard_map/while/body/eval_jaxpr/sub | solution.py:181
  594.6 38.1 %reduce-scatter.42.cloned.1.call-done = bf16[3,512,256]{2,1,0:T(8,128)(2,1)} async-done(((bf16[3,512,1024]{2,1,0:T(8,128)(2,1)}), bf16[3,512,256]{2,1,0:T(8,128)(2,1)}) %reduce-scatter.42.cloned.1.call-update) | async-done | bytes 786448 | tf_op jit(solution)/shard_map/reduce_scatter | solution.py:41
  728.1 22.3 %fusion.2 = f32[512,32,3,4]{1,3,2,0:T(4,128)} fusion(f32[3,4,512,512]{3,1,0,2:T(4,128)} %copy.287, s32[512,512]{1,0:T(8,128)S(1)} %copy-done.53), kind=kOutput, calls=%fused_computation.3 | convolution fusion | flops 1216348160 | bytes 14417920 | tf_op jit(solution)/shard_map/while/body/eval_jaxpr/nhts,tsb->nthb/dot_general | solution.py:152
  824.8 24.8 %reduce-scatter.46.cloned.1.call-done = bf16[512,256]{1,0:T(8,128)(2,1)} async-done(((bf16[512,1024]{1,0:T(8,128)(2,1)}), bf16[512,256]{1,0:T(8,128)(2,1)}) %reduce-scatter.46.cloned.1.call-update) | async-done | bytes 262160 | tf_op jit(solution)/shard_map/reduce_scatter | solution.py:380
  851.3 67.0 %reduce-scatter.48.cloned.1.call-done = bf16[3,128,256]{2,1,0:T(8,128)(2,1)} async-done(((bf16[3,1024,256]{2,1,0:T(8,128)(2,1)}), bf16[3,128,256]{2,1,0:T(8,128)(2,1)}) %reduce-scatter.48.cloned.1.call-update) | async-done | bytes 196624 | tf_op jit(solution)/shard_map/reduce_scatter | solution.py:441
  920.0 61.7 %reduce-scatter.62.cloned.1.call-done = f32[32,3]{1,0:T(8,128)} async-done(((f32[256,3]{1,0:T(8,128)}), f32[32,3]{1,0:T(8,128)}) %reduce-scatter.62.cloned.1.call-update) | async-done | bytes 400
  983.1 62.1 %reduce-scatter.66.cloned.1.call-done = f32[32,3]{1,0:T(8,128)} async-done(((f32[256,3]{1,0:T(8,128)}), f32[32,3]{1,0:T(8,128)}) %reduce-scatter.66.cloned.1.call-update) | async-done | bytes 400
  1046.5 62.2 %reduce-scatter.64.cloned.1.call-done = f32[32,3]{1,0:T(8,128)} async-done(((f32[256,3]{1,0:T(8,128)}), f32[32,3]{1,0:T(8,128)}) %reduce-scatter.64.cloned.1.call-update) | async-done | bytes 400
  1111.3 19.7 %all-reduce.2 = (f32[128]{0:T(128)S(1)}, f32[1024]{0:T(1024)S(1)}) all-reduce(f32[128]{0:T(128)S(1)} %reduce_sum.369, f32[1024]{0:T(1024)S(1)} %copy-done.78), channel_id=16, replica_groups=mesh['tensor'=4,'batch'=8] {'batch'}, use_global_device_ids=true, to_apply=%region_54.56.clone | all-reduce | flops 1152 | bytes 9216
  1132.2 40.1 %reduce-scatter.60.cloned.1.call-done = f32[32,4]{1,0:T(8,128)} async-done(((f32[256,4]{1,0:T(8,128)}), f32[32,4]{1,0:T(8,128)}) %reduce-scatter.60.cloned.1.call-update) | async-done | bytes 528
  1173.6 62.7 %reduce-scatter.54.cloned.1.call-done = bf16[128,128]{1,0:T(8,128)(2,1)} async-done(((bf16[1024,128]{1,0:T(8,128)(2,1)}), bf16[128,128]{1,0:T(8,128)(2,1)}) %reduce-scatter.54.cloned.1.call-update) | async-done | bytes 32784
  1237.9 64.6 %reduce-scatter.56.cloned.1.call-done = bf16[128,512]{1,0:T(8,128)(2,1)} async-done(((bf16[1024,512]{1,0:T(8,128)(2,1)}), bf16[128,512]{1,0:T(8,128)(2,1)}) %reduce-scatter.56.cloned.1.call-update) | async-done | bytes 131088
  1304.3 65.5 %reduce-scatter.52.cloned.1.call-done = bf16[128,768]{1,0:T(8,128)(2,1)} async-done(((bf16[1024,768]{1,0:T(8,128)(2,1)}), bf16[128,768]{1,0:T(8,128)(2,1)}) %reduce-scatter.52.cloned.1.call-update) | async-done | bytes 196624
  1372.0 37.3 %reduce-scatter.44.cloned.1.call-done = bf16[3,512,256]{2,1,0:T(8,128)(2,1)} async-done(((bf16[3,512,1024]{2,1,0:T(8,128)(2,1)}), bf16[3,512,256]{2,1,0:T(8,128)(2,1)}) %reduce-scatter.44.cloned.1.call-update) | async-done | bytes 786448 | tf_op jit(solution)/shard_map/reduce_scatter | solution.py:41
  (454 shorter events, 454.6 us)
Async XLA Ops:
  7.2 34.1 %all-gather.8.cloned.1.call-start = ((), (), s32[]{:S(2)}) async-start(), calls=%async_computation.17 | async-start | bytes 3932160 | tf_op jit(solution)/shard_map/all_gather | solution.py:37
  7.9 157.3 %reduce-scatter.34.cloned.1.call-start = ((), (), s32[]{:S(2)}) async-start(), calls=%async_computation.18 | async-start | bytes 3932160 | tf_op jit(solution)/shard_map/reduce_scatter | solution.py:41
  127.2 56.9 %all-gather.10.cloned.1.call-start = ((), (), s32[]{:S(2)}) async-start(), calls=%async_computation.19 | async-start | bytes 1310720 | tf_op jit(solution)/shard_map/all_gather | solution.py:315
  127.9 87.1 %all-gather.12.cloned.1.call-start = ((), (), s32[]{:S(2)}) async-start(), calls=%async_computation.20 | async-start | bytes 3932160 | tf_op jit(solution)/shard_map/all_gather | solution.py:37
  183.3 87.9 %reduce-scatter.36.cloned.1.call-start = ((), (), s32[]{:S(2)}) async-start(), calls=%async_computation.21 | async-start | bytes 3932160 | tf_op jit(solution)/shard_map/reduce_scatter | solution.py:41
  233.1 88.2 %all-gather.14.cloned.1.call-start = ((), (), s32[]{:S(2)}) async-start(), calls=%async_computation.22 | async-start | bytes 3932160 | tf_op jit(solution)/shard_map/all_gather | solution.py:37
  290.8 98.0 %reduce-scatter.38.cloned.1.call-start = ((), (), s32[]{:S(2)}) async-start(), calls=%async_computation.23 | async-start | bytes 3932160 | tf_op jit(solution)/shard_map/reduce_scatter | solution.py:41
  350.7 104.3 %all-gather.16.cloned.1.call-start = ((), (), s32[]{:S(2)}) async-start(), calls=%async_computation.24 | async-start | bytes 3932160 | tf_op jit(solution)/shard_map/all_gather | solution.py:37
  426.0 86.4 %reduce-scatter.40.cloned.1.call-start = ((), (), s32[]{:S(2)}) async-start(), calls=%async_computation.25 | async-start | bytes 3932160 | tf_op jit(solution)/shard_map/reduce_scatter | solution.py:41
  474.3 84.6 %all-gather.18.cloned.1.call-start = ((), (), s32[]{:S(2)}) async-start(), calls=%async_computation.26 | async-start | bytes 3932160 | tf_op jit(solution)/shard_map/all_gather | solution.py:37
  528.7 104.0 %reduce-scatter.42.cloned.1.call-start = ((), (), s32[]{:S(2)}) async-start(), calls=%async_computation.27 | async-start | bytes 3932160 | tf_op jit(solution)/shard_map/reduce_scatter | solution.py:41
  594.5 95.9 %all-gather.20.cloned.1.call-start = ((), (), s32[]{:S(2)}) async-start(), calls=%async_computation.28 | async-start | bytes 3932160 | tf_op jit(solution)/shard_map/all_gather | solution.py:37
  650.3 159.6 %reduce-scatter.58.cloned.1.call-start = ((), (), s32[]{:S(2)}) async-start(), calls=%async_computation.36 | async-start | bytes 2359296
  659.6 163.4 %reduce-scatter.50.cloned.1.call-start = ((), (), s32[]{:S(2)}) async-start(), calls=%async_computation.32 | async-start | bytes 2359296 | tf_op jit(solution)/shard_map/reduce_scatter | solution.py:441
  667.5 182.0 %reduce-scatter.46.cloned.1.call-start = ((), (), s32[]{:S(2)}) async-start(), calls=%async_computation.30 | async-start | bytes 1310720 | tf_op jit(solution)/shard_map/reduce_scatter | solution.py:380
  681.5 236.9 %reduce-scatter.48.cloned.1.call-start = ((), (), s32[]{:S(2)}) async-start(), calls=%async_computation.31 | async-start | bytes 1769472 | tf_op jit(solution)/shard_map/reduce_scatter | solution.py:441
  686.3 295.4 %reduce-scatter.62.cloned.1.call-start = ((), (), s32[]{:S(2)}) async-start(), calls=%async_computation.38 | async-start | bytes 147456
  688.1 357.0 %reduce-scatter.66.cloned.1.call-start = ((), (), s32[]{:S(2)}) async-start(), calls=%async_computation.40 | async-start | bytes 147456
  689.0 419.7 %reduce-scatter.64.cloned.1.call-start = ((), (), s32[]{:S(2)}) async-start(), calls=%async_computation.39 | async-start | bytes 147456
  690.0 482.3 %reduce-scatter.60.cloned.1.call-start = ((), (), s32[]{:S(2)}) async-start(), calls=%async_computation.37 | async-start | bytes 147456
  767.9 468.4 %reduce-scatter.54.cloned.1.call-start = ((), (), s32[]{:S(2)}) async-start(), calls=%async_computation.34 | async-start | bytes 294912
  773.0 529.6 %reduce-scatter.56.cloned.1.call-start = ((), (), s32[]{:S(2)}) async-start(), calls=%async_computation.35 | async-start | bytes 1179648
  784.4 585.4 %reduce-scatter.52.cloned.1.call-start = ((), (), s32[]{:S(2)}) async-start(), calls=%async_computation.33 | async-start | bytes 1769472
  799.2 610.2 %reduce-scatter.44.cloned.1.call-start = ((), (), s32[]{:S(2)}) async-start(), calls=%async_computation.29 | async-start | bytes 3932160 | tf_op jit(solution)/shard_map/reduce_scatter | solution.py:41
  (96 other events, 1840.9 us)
Sparse Core Ops, SparseCore 0:
  9.6 31.6 all-gather.7
  127.3 37.9 reduce-scatter.33
  166.9 17.0 all-gather.9
  186.1 28.9 all-gather.11
  233.3 37.9 reduce-scatter.35
  291.0 30.3 all-gather.13
  350.9 37.9 reduce-scatter.37
  426.1 28.9 all-gather.15
  474.4 37.9 reduce-scatter.39
  528.8 30.0 all-gather.17
  594.6 37.9 reduce-scatter.41
  650.4 29.9 all-gather.19
  684.4 67.9 reduce-scatter.57
  756.1 66.7 reduce-scatter.49
  825.5 23.9 reduce-scatter.45
  852.8 65.4 reduce-scatter.47
  921.8 59.8 reduce-scatter.61
  985.2 59.8 reduce-scatter.65
  1048.8 59.8 reduce-scatter.63
  1112.3 59.9 reduce-scatter.59
  1175.9 60.2 reduce-scatter.53
  1240.1 62.4 reduce-scatter.55
  1305.9 63.8 reduce-scatter.51
  1372.4 36.8 reduce-scatter.43
